TPU v7x, 32 devices: a whole 2x2x4 slice. The times are simulated.
32 devices in a mesh: groups: 2 (over y), pipe: 4 (over z), hour: 2 (over x), seg: 2 (over core).
Axes of the slice: x: 2, y: 2, z: 4, core: 2. Of those that a mesh axis runs over, the one named last changes fastest.
Arguments:
- segment_flow: float32 [16, 64, 1024], P(('groups', 'hour'), 'seg', 'pipe'), parts along dimension 0, may hold values from -4 to 4
- linepack: float32 [16, 64, 1024], P(('groups', 'hour'), 'seg', 'pipe'), parts along dimension 0, may hold values from 0.2 to 2.4
- mass_dual: float32 [16, 64, 1024], P(('groups', 'hour'), 'seg', 'pipe'), parts along dimension 0, may hold values from -3 to 3
- momentum_dual: float32 [16, 64, 1024], P(('groups', 'hour'), 'seg', 'pipe'), parts along dimension 0, may hold values from -3 to 3
- contract_dual: float32 [16, 2, 32, 128], P(('groups', 'hour'), 'seg', 'pipe'), parts along dimension 0, may hold values from -3 to 3
- flow_cost: float32 [16, 64, 1024], P(('groups', 'hour'), 'seg', 'pipe'), parts along dimension 0, may hold values from -24 to 24
- injection: float32 [16, 64, 1024], P(('groups', 'hour'), 'seg', 'pipe'), parts along dimension 0, may hold values from -3 to 3
- contract_target: float32 [16, 2, 32, 128], P(('groups', 'hour'), 'seg', 'pipe'), parts along dimension 0, may hold values from 0.4 to 2
- friction_table: float32 [16], replicated, may hold values from 0.3 to 3
- friction_class: int32 [64, 2048], P('seg', ('groups', 'pipe')), parts along dimension 1, may hold values from 0 to 15
- matching: int32 [2048], P('groups'), parts along dimension 0, may hold values from 0 to 1023, as said below
- contract_map: int32 [16, 1024], P(('groups', 'hour')), parts along dimension 0, may hold values from 0 to 127
Outputs:
- flow_final: float32 [16, 64, 1024], P(('groups', 'hour'), 'seg', 'pipe'), parts along dimension 0
- linepack_final: float32 [16, 64, 1024], P(('groups', 'hour'), 'seg', 'pipe'), parts along dimension 0
- mass_dual_final: float32 [16, 64, 1024], P(('groups', 'hour'), 'seg', 'pipe'), parts along dimension 0
- momentum_dual_final: float32 [16, 64, 1024], P(('groups', 'hour'), 'seg', 'pipe'), parts along dimension 0
- contract_dual_final: float32 [16, 2, 32, 128], P(('groups', 'hour'), 'seg', 'pipe'), parts along dimension 0
- primal_weight: float32 [2], P('groups'), parts along dimension 0
There are 2 independent parts, one for each index of `groups`. A program takes and returns all parts, laid end to end along the dimension named above; an argument that names none is the same for every part. Nothing has to cross between parts.
Inputs may be any that keep to these rules, and one draw needn't show every extreme that they name: `matching`: every pipe's inlet is fed by the outlet of exactly one pipe: each number of 0 to 1023 appears once; for any two blocks of 256 consecutive pipes, exactly 64 pipes of the first are fed from outlets of the second.
All inputs are finite; a program needn't handle non-finite values.
Results may differ from a plain program's by a relative error of at most 0.0001.
Values sent between devices are 32-bit elements; how exact they have to be, the bound alone decides.
A program may use at most 64 MiB of HBM per device.

v0:
```python
import math
import jax
import jax.numpy as jnp
from jax import lax
from jax.sharding import PartitionSpec as P

ITERS = 2
FLOW_CAP = 1.5
PACK_CAP = 2.5
STEP_SCALE = 0.25
NORM_EPS = 1e-06


def padded(cells, sides, width):
    for axis, dim in sides:
        count = lax.axis_size(axis)
        ends = count - 1
        head = lax.slice_in_dim(cells, 0, width, axis=dim)
        tail = lax.slice_in_dim(cells, cells.shape[dim] - width, cells.shape[dim], axis=dim)
        cells = jnp.concatenate(
            [
                lax.ppermute(tail, axis, [(i, (i + 1) % count) for i in range(ends)]),
                cells,
                lax.ppermute(head, axis, [((i + 1) % count, i) for i in range(ends)]),
            ],
            axis=dim,
        )
    return cells


def widened_pair(stacked):
    return padded(stacked, (("hour", 1), ("seg", 2)), 1)


def other_half(edge_row, half_index, partner_local):
    gathered = lax.all_gather(edge_row[:, None, :], ("pipe", "seg"), axis=1, tiled=True)
    hour_rows, row_count, row_width = gathered.shape
    seg_count = lax.axis_size("seg")
    picked = gathered.reshape(hour_rows, row_count // seg_count, seg_count, row_width)[
        :, :, half_index, :
    ]
    far_rows = picked.reshape(hour_rows, row_count // seg_count * row_width)
    return jnp.take(far_rows, partner_local, axis=1)


def contract_local(values, contract_rows, class_count):
    hour_rows, seg_rows, pipe_rows = values.shape
    block = math.gcd(pipe_rows, 2048)
    classes = jnp.arange(class_count, dtype=jnp.int32)

    def add_block(block_index, total):
        partial_value = lax.dynamic_slice_in_dim(values, block_index * block, block, 2)
        row_map = lax.dynamic_slice_in_dim(contract_rows, block_index * block, block, 1)
        onehot = (row_map[:, :, None] == classes[None, None, :]).astype(jnp.float32)
        return total + jnp.einsum(
            "hsp,hpc->hsc",
            partial_value,
            onehot,
            precision=lax.Precision.HIGHEST,
            preferred_element_type=jnp.float32,
        )

    return lax.fori_loop(
        0, pipe_rows // block, add_block, jnp.zeros((hour_rows, seg_rows, class_count), jnp.float32)
    )


def spread_local(duals, contract_rows):
    hour_rows, seg_rows, class_count = duals.shape
    pipe_rows = contract_rows.shape[1]
    block = math.gcd(pipe_rows, 2048)
    classes = jnp.arange(class_count, dtype=jnp.int32)

    def fill_block(block_index, result_now):
        row_map = lax.dynamic_slice_in_dim(contract_rows, block_index * block, block, 1)
        onehot = (row_map[:, :, None] == classes[None, None, :]).astype(jnp.float32)
        partial_value = jnp.einsum(
            "hsc,hpc->hsp",
            duals,
            onehot,
            precision=lax.Precision.HIGHEST,
            preferred_element_type=jnp.float32,
        )
        return lax.dynamic_update_slice_in_dim(result_now, partial_value, block_index * block, 2)

    return lax.fori_loop(
        0, pipe_rows // block, fill_block, jnp.zeros((hour_rows, seg_rows, pipe_rows), jnp.float32)
    )


def on_device(
    segment_flow,
    linepack,
    mass_dual,
    momentum_dual,
    contract_dual,
    flow_cost,
    injection,
    contract_target,
    friction_table,
    friction_class,
    matching,
    contract_map,
):
    hour_rows, seg_rows, pipe_rows = segment_flow.shape
    class_count = contract_dual.shape[3]
    pipe_count = lax.axis_size("pipe")
    total_pipes = pipe_rows * pipe_count
    share_scale = class_count / total_pipes
    pipe_start = lax.axis_index("pipe") * pipe_rows
    seg_index = lax.axis_index("seg")
    at_start = seg_index == 0
    at_end = seg_index == lax.axis_size("seg") - 1
    levels = jnp.arange(friction_table.shape[0], dtype=jnp.int32)
    friction = jnp.sum(
        jnp.where(
            friction_class[None] == levels[:, None, None], friction_table[:, None, None], 0.0
        ),
        axis=0,
    )[None]
    inverse = (
        jnp.zeros_like(matching).at[matching].set(jnp.arange(matching.shape[0], dtype=jnp.int32))
    )
    source_local = lax.dynamic_slice_in_dim(matching, pipe_start, pipe_rows)
    target_local = lax.dynamic_slice_in_dim(inverse, pipe_start, pipe_rows)
    contract_now = contract_dual.reshape(hour_rows, contract_dual.shape[2], class_count)
    target_now = contract_target.reshape(hour_rows, contract_target.shape[2], class_count)
    weight = jnp.float32(1.0)
    for iteration in range(ITERS):
        primal_step = STEP_SCALE / weight
        dual_step = STEP_SCALE * weight
        widened = widened_pair(jnp.stack([mass_dual, momentum_dual]))
        last_base = widened[0, 1:-1, -1, :]
        later_hour = widened[0, 2:, 1:-1, :]
        before_seg = widened[1, 1:-1, :-2, :]
        returned = other_half(mass_dual[:, 0, :], 0, target_local)
        last_row = last_base + jnp.where(at_end, returned, 0.0)
        next_seg = jnp.concatenate([mass_dual[:, 1:, :], last_row[:, None, :]], axis=1)
        grad_flow = mass_dual - next_seg + friction * momentum_dual
        hour_spread = spread_local(contract_now, contract_map)
        spread = lax.all_to_all(hour_spread, "pipe", split_axis=2, concat_axis=1, tiled=True)
        grad_pack = mass_dual - later_hour - momentum_dual + before_seg + share_scale * spread
        grad_flow, grad_pack = (grad_flow, grad_pack)
        flow_next = jnp.clip(
            segment_flow - primal_step * (flow_cost - grad_flow), -FLOW_CAP, FLOW_CAP
        )
        pack_next = jnp.clip(linepack + primal_step * grad_pack, 0.0, PACK_CAP)
        flow_bar = 2.0 * flow_next - segment_flow
        pack_bar = 2.0 * pack_next - linepack
        forward_widened = widened_pair(jnp.stack([flow_bar, pack_bar]))
        first_base = forward_widened[0, 1:-1, 0, :]
        earlier = forward_widened[1, :-2, 1:-1, :]
        after_seg = forward_widened[1, 1:-1, 2:, :]
        inflow = other_half(flow_bar[:, -1, :], 1, source_local)
        first_row = first_base + jnp.where(at_start, inflow, 0.0)
        upstream = jnp.concatenate([first_row[:, None, :], flow_bar[:, :-1, :]], axis=1)
        mass_rows = pack_bar - earlier + flow_bar - upstream
        momentum = friction * flow_bar - (pack_bar - after_seg)
        hour_major = lax.all_to_all(pack_bar, "pipe", split_axis=1, concat_axis=2, tiled=True)
        totals = contract_local(hour_major, contract_map, class_count)
        mass_rows, momentum, totals = (mass_rows, momentum, share_scale * totals)
        mass_next = mass_dual + dual_step * (injection - mass_rows)
        momentum_next = momentum_dual - dual_step * momentum
        contract_next = contract_now + dual_step * (target_now - totals)
        primal_sq = jnp.sum((flow_next - segment_flow) ** 2) + jnp.sum((pack_next - linepack) ** 2)
        dual_sq = (
            jnp.sum((mass_next - mass_dual) ** 2)
            + jnp.sum((momentum_next - momentum_dual) ** 2)
            + jnp.sum((contract_next - contract_now) ** 2)
        )
        primal_total, dual_total = lax.psum((primal_sq, dual_sq), ("pipe", "hour", "seg"))
        weight = jnp.sqrt(weight * jnp.sqrt((dual_total + NORM_EPS) / (primal_total + NORM_EPS)))
        segment_flow, linepack = (flow_next, pack_next)
        mass_dual, momentum_dual, contract_now = (mass_next, momentum_next, contract_next)
    return (
        segment_flow,
        linepack,
        mass_dual,
        momentum_dual,
        contract_now.reshape(contract_dual.shape),
        weight.reshape(1),
    )


def solution(mesh):
    return jax.shard_map(
        on_device,
        mesh=mesh,
        in_specs=(
            P(("groups", "hour"), "seg", "pipe"),
            P(("groups", "hour"), "seg", "pipe"),
            P(("groups", "hour"), "seg", "pipe"),
            P(("groups", "hour"), "seg", "pipe"),
            P(("groups", "hour"), "seg", "pipe", None),
            P(("groups", "hour"), "seg", "pipe"),
            P(("groups", "hour"), "seg", "pipe"),
            P(("groups", "hour"), "seg", "pipe", None),
            P(),
            P("seg", ("groups", "pipe")),
            P("groups"),
            P(("groups", "hour"), None),
        ),
        out_specs=(
            P(("groups", "hour"), "seg", "pipe"),
            P(("groups", "hour"), "seg", "pipe"),
            P(("groups", "hour"), "seg", "pipe"),
            P(("groups", "hour"), "seg", "pipe"),
            P(("groups", "hour"), "seg", "pipe", None),
            P("groups"),
        ),
        check_vma=False,
    )
```

profile of v0, /device:TPU:0, one launch (start us, length us, event | category | flops | bytes accessed | tf_op | source)
XLA Modules:
  0.0 255.9 jit_solution(9958504613072737630)
XLA Ops:
  3.7 3.1 %reshape.116 = f32[4,1,8192]{2,1,0:T(1,128)} reshape(f32[1024,4,8]{2,1,0:T(4,128)S(1)} %bitcast.195) | data formatting | bytes 262144
  6.8 6.3 %all-to-all-start = ((f32[4,1,8192]{2,1,0:T(1,128)}), f32[4,1,8192]{2,1,0:T(1,128)S(1)}, u32[]{:S(2)}, u32[]{:S(2)}) async-start(f32[4,1,8192]{2,1,0:T(1,128)} %reshape.116), calls=%async_computation | async-start | bytes 262144 | tf_op jit(solution)/shard_map/all_to_all | solution.py:141
  14.5 4.5 %collective-permute-start = (f32[2,1,32,256]{3,2,1,0:T(8,128)S(1)}, f32[2,1,32,256]{3,2,1,0:T(8,128)S(1)}, u32[]{:S(2)}, u32[]{:S(2)}) collective-permute-start(f32[2,1,32,256]{3,2,1,0:T(8,128)S(1)} %get-tuple-element.135), channel_id=1, source_target_pairs={{0,2},{1,3},{4,6},{5,7},{8,10},{9,11},{12,14},{13,15},{16,18},{17,... | collective-permute-start | bytes 196616 | tf_op jit(solution)/shard_map/ppermute | solution.py:22
  19.1 14.6 %all_gather.12 = f32[4,8,256]{2,0,1:T(4,128)S(1)} all-gather(f32[4,1,256]{2,0,1:T(4,128)S(1)} %copy.255), channel_id=1, replica_groups=mesh['groups'=2,'pipe'=4,'hour'=2,'seg'=2] {'pipe','seg'}, dimensions={1}, use_global_device_ids=true | all-gather | bytes 36864 | tf_op jit(solution)/shard_map/all_gather | solution.py:36
  33.9 4.3 %scatter_custom_fusion = s32[1024]{0:T(1024)S(1)} fusion(s32[1024]{0:T(1024)S(1)} %compare_select_fusion, s32[1024]{0:T(1024)S(1)} %iota.14, s32[]{:T(128)} %constant.26.clone.1), kind=kCustom, calls=%fused_computation.140 | custom fusion | bytes 4100 | tf_op jit(solution)/shard_map/scatter | solution.py:122
  40.3 2.2 collective-permute-start.3
  47.8 2.5 reshape.117
  58.7 4.5 %collective-permute-start.4 = (f32[2,1,32,256]{3,2,1,0:T(8,128)S(1)}, f32[2,1,32,256]{3,2,1,0:T(8,128)S(1)}, u32[]{:S(2)}, u32[]{:S(2)}) collective-permute-start(f32[2,1,32,256]{3,2,1,0:T(8,128)S(1)} %get-tuple-element.131), channel_id=1, source_target_pairs={{0,2},{1,3},{4,6},{5,7},{8,10},{9,11},{12,14},{13,15},{16,18},{17,... | collective-permute-start | bytes 196616 | tf_op jit(solution)/shard_map/ppermute | solution.py:22
  63.3 14.0 %all_gather.13 = f32[4,8,256]{2,0,1:T(4,128)S(1)} all-gather(f32[4,1,256]{2,0,1:T(4,128)S(1)} %slice.182), channel_id=1, replica_groups=mesh['groups'=2,'pipe'=4,'hour'=2,'seg'=2] {'pipe','seg'}, dimensions={1}, use_global_device_ids=true | all-gather | bytes 36864 | tf_op jit(solution)/shard_map/all_gather | solution.py:36
  78.7 2.2 collective-permute-start.6
  87.5 4.5 %collective-permute-start.8 = (f32[2,1,32,256]{3,2,1,0:T(8,128)S(1)}, f32[2,1,32,256]{3,2,1,0:T(8,128)S(1)}, u32[]{:S(2)}, u32[]{:S(2)}) collective-permute-start(f32[2,1,32,256]{3,2,1,0:T(8,128)S(1)} %get-tuple-element.127), channel_id=1, source_target_pairs={{0,2},{1,3},{4,6},{5,7},{8,10},{9,11},{12,14},{13,15},{16,18},{17,... | collective-permute-start | bytes 196616 | tf_op jit(solution)/shard_map/ppermute | solution.py:22
  92.0 4.5 %all-to-all-start.1 = ((f32[4,32,256]{2,0,1:T(4,128)}), f32[4,32,256]{2,0,1:T(4,128)S(1)}, u32[]{:S(2)}, u32[]{:S(2)}) async-start(f32[4,32,256]{2,0,1:T(4,128)} %multiply_subtract_fusion.3), calls=%async_computation.1 | async-start | bytes 262144 | tf_op jit(solution)/shard_map/all_to_all | solution.py:159
  98.5 14.6 %all_gather.14 = f32[4,8,256]{2,0,1:T(4,128)S(1)} all-gather(f32[4,1,256]{2,0,1:T(4,128)S(1)} %slice.191), channel_id=1, replica_groups=mesh['groups'=2,'pipe'=4,'hour'=2,'seg'=2] {'pipe','seg'}, dimensions={1}, use_global_device_ids=true | all-gather | bytes 36864 | tf_op jit(solution)/shard_map/all_gather | solution.py:36
  120.7 2.2 fusion.73
  125.6 3.1 %reshape.118 = f32[4,1,8192]{2,1,0:T(1,128)} reshape(f32[1024,4,8]{2,1,0:T(4,128)S(1)} %bitcast.197) | data formatting | bytes 262144
  128.7 4.5 %all-to-all-start.2 = ((f32[4,1,8192]{2,1,0:T(1,128)}), f32[4,1,8192]{2,1,0:T(1,128)S(1)}, u32[]{:S(2)}, u32[]{:S(2)}) async-start(f32[4,1,8192]{2,1,0:T(1,128)} %reshape.118), calls=%async_computation.2 | async-start | bytes 262144 | tf_op jit(solution)/shard_map/all_to_all | solution.py:141
  135.1 33.5 %all-reduce.1 = (f32[]{:T(128)}, f32[]{:T(128)}) all-reduce(f32[]{:T(128)S(6)} %add.153, f32[]{:T(128)S(6)} %add.155), channel_id=1, replica_groups=mesh['groups'=2,'pipe'=4,'hour'=2,'seg'=2] {'pipe','hour','seg'}, use_global_device_ids=true, to_apply=%region_5.7 | all-reduce | flops 2 | bytes 16 | tf_op jit(solution)/shard_map/psum | solution.py:171
  171.0 2.5 reshape.119
  181.3 4.5 %collective-permute-start.12 = (f32[2,1,32,256]{3,2,1,0:T(8,128)S(1)}, f32[2,1,32,256]{3,2,1,0:T(8,128)S(1)}, u32[]{:S(2)}, u32[]{:S(2)}) collective-permute-start(f32[2,1,32,256]{3,2,1,0:T(8,128)S(1)} %get-tuple-element.123), channel_id=1, source_target_pairs={{0,2},{1,3},{4,6},{5,7},{8,10},{9,11},{12,14},{13,15},{16,18},{17,... | collective-permute-start | bytes 196616 | tf_op jit(solution)/shard_map/ppermute | solution.py:22
  187.2 3.5 %all-to-all-start.3 = ((f32[4,32,256]{2,0,1:T(4,128)}), f32[4,32,256]{2,0,1:T(4,128)S(1)}, u32[]{:S(2)}, u32[]{:S(2)}) async-start(f32[4,32,256]{2,0,1:T(4,128)} %multiply_subtract_fusion.1), calls=%async_computation.3 | async-start | bytes 262144 | tf_op jit(solution)/shard_map/all_to_all | solution.py:159
  190.7 14.6 %all_gather.15 = f32[4,8,256]{2,0,1:T(4,128)S(1)} all-gather(f32[4,1,256]{2,0,1:T(4,128)S(1)} %slice.198), channel_id=1, replica_groups=mesh['groups'=2,'pipe'=4,'hour'=2,'seg'=2] {'pipe','seg'}, dimensions={1}, use_global_device_ids=true | all-gather | bytes 36864 | tf_op jit(solution)/shard_map/all_gather | solution.py:36
  209.4 3.0 %collective-permute-start.14 = (f32[2,6,1,256]{1,3,2,0:T(8,128)S(1)}, f32[2,6,1,256]{1,3,2,0:T(8,128)S(1)}, u32[]{:S(2)}, u32[]{:S(2)}) collective-permute-start(f32[2,6,1,256]{1,3,2,0:T(8,128)S(1)} %copy.201), channel_id=1, source_target_pairs={{0,1},{2,3},{4,5},{6,7},{8,9},{10,11},{12,13},{14,15},{16,17},{18,... | collective-permute-start | bytes 36872 | tf_op jit(solution)/shard_map/ppermute | solution.py:22
  217.6 2.4 multiply_reduce_fusion.8
  221.4 32.0 %all-reduce = (f32[]{:T(128)}, f32[]{:T(128)}) all-reduce(f32[]{:T(128)S(6)} %add.167, f32[]{:T(128)S(6)} %add.169), channel_id=1, replica_groups=mesh['groups'=2,'pipe'=4,'hour'=2,'seg'=2] {'pipe','hour','seg'}, use_global_device_ids=true, to_apply=%region_12.14 | all-reduce | flops 2 | bytes 16 | tf_op jit(solution)/shard_map/psum | solution.py:171
  (159 shorter events, 56.0 us)
Async XLA Ops:
  3.7 35.3 %copy-start.11 = (s32[32,256]{1,0:T(8,128)S(1)}, s32[32,256]{1,0:T(8,128)}, u32[]{:S(2)}) copy-start(s32[32,256]{1,0:T(8,128)} %param.23) | copy-start | bytes 98308
  3.7 35.3 %copy-start.13 = (f32[16]{0:T(128)S(1)}, f32[16]{0:T(128)}, u32[]{:S(2)}) copy-start(f32[16]{0:T(128)} %param.22) | copy-start | bytes 196
  6.8 39.5 %all-to-all-start = ((f32[4,1,8192]{2,1,0:T(1,128)}), f32[4,1,8192]{2,1,0:T(1,128)S(1)}, u32[]{:S(2)}, u32[]{:S(2)}) async-start(f32[4,1,8192]{2,1,0:T(1,128)} %reshape.116), calls=%async_computation | async-start | bytes 262144 | tf_op jit(solution)/shard_map/all_to_all | solution.py:141
  13.2 26.8 %collective-permute-start.1 = (f32[2,1,32,256]{3,2,1,0:T(8,128)S(1)}, f32[2,1,32,256]{3,2,1,0:T(8,128)S(1)}, u32[]{:S(2)}, u32[]{:S(2)}) collective-permute-start(f32[2,1,32,256]{3,2,1,0:T(8,128)S(1)} %get-tuple-element.136), channel_id=1, source_target_pairs={{2,0},{3,1},{6,4},{7,5},{10,8},{11,9},{14,12},{15,13},{18,16},{19,... | collective-permute-start | bytes 196616 | tf_op jit(solution)/shard_map/ppermute | solution.py:24
  14.5 25.5 %collective-permute-start = (f32[2,1,32,256]{3,2,1,0:T(8,128)S(1)}, f32[2,1,32,256]{3,2,1,0:T(8,128)S(1)}, u32[]{:S(2)}, u32[]{:S(2)}) collective-permute-start(f32[2,1,32,256]{3,2,1,0:T(8,128)S(1)} %get-tuple-element.135), channel_id=1, source_target_pairs={{0,2},{1,3},{4,6},{5,7},{8,10},{9,11},{12,14},{13,15},{16,18},{17,... | collective-permute-start | bytes 196616 | tf_op jit(solution)/shard_map/ppermute | solution.py:22
  40.3 13.8 %collective-permute-start.3 = (f32[2,6,1,256]{3,1,2,0:T(8,128)S(1)}, f32[2,6,1,256]{3,1,2,0:T(8,128)S(1)}, u32[]{:S(2)}, u32[]{:S(2)}) collective-permute-start(f32[2,6,1,256]{3,1,2,0:T(8,128)S(1)} %slice.177), channel_id=1, source_target_pairs={{0,1},{2,3},{4,5},{6,7},{8,9},{10,11},{12,13},{14,15},{16,17},{18,... | collective-permute-start | bytes 36872 | tf_op jit(solution)/shard_map/ppermute | solution.py:22
  42.7 3.4 %collective-permute-start.2 = (f32[2,6,1,256]{1,3,2,0:T(8,128)S(1)}, f32[2,6,1,256]{1,3,2,0:T(8,128)S(1)}, u32[]{:S(2)}, u32[]{:S(2)}) collective-permute-start(f32[2,6,1,256]{1,3,2,0:T(8,128)S(1)} %copy.191), channel_id=1, source_target_pairs={{1,0},{3,2},{5,4},{7,6},{9,8},{11,10},{13,12},{15,14},{17,16},{19,... | collective-permute-start | bytes 36872 | tf_op jit(solution)/shard_map/ppermute | solution.py:24
  57.2 21.0 %collective-permute-start.5 = (f32[2,1,32,256]{3,2,1,0:T(8,128)S(1)}, f32[2,1,32,256]{3,2,1,0:T(8,128)S(1)}, u32[]{:S(2)}, u32[]{:S(2)}) collective-permute-start(f32[2,1,32,256]{3,2,1,0:T(8,128)S(1)} %get-tuple-element.132), channel_id=1, source_target_pairs={{2,0},{3,1},{6,4},{7,5},{10,8},{11,9},{14,12},{15,13},{18,16},{19,... | collective-permute-start | bytes 196616 | tf_op jit(solution)/shard_map/ppermute | solution.py:24
  58.7 19.6 %collective-permute-start.4 = (f32[2,1,32,256]{3,2,1,0:T(8,128)S(1)}, f32[2,1,32,256]{3,2,1,0:T(8,128)S(1)}, u32[]{:S(2)}, u32[]{:S(2)}) collective-permute-start(f32[2,1,32,256]{3,2,1,0:T(8,128)S(1)} %get-tuple-element.131), channel_id=1, source_target_pairs={{0,2},{1,3},{4,6},{5,7},{8,10},{9,11},{12,14},{13,15},{16,18},{17,... | collective-permute-start | bytes 196616 | tf_op jit(solution)/shard_map/ppermute | solution.py:22
  78.7 3.7 %collective-permute-start.6 = (f32[2,6,1,256]{1,3,2,0:T(8,128)S(1)}, f32[2,6,1,256]{1,3,2,0:T(8,128)S(1)}, u32[]{:S(2)}, u32[]{:S(2)}) collective-permute-start(f32[2,6,1,256]{1,3,2,0:T(8,128)S(1)} %copy.195), channel_id=1, source_target_pairs={{0,1},{2,3},{4,5},{6,7},{8,9},{10,11},{12,13},{14,15},{16,17},{18,... | collective-permute-start | bytes 36872 | tf_op jit(solution)/shard_map/ppermute | solution.py:22
  81.0 3.1 %collective-permute-start.7 = (f32[2,6,1,256]{3,1,2,0:T(8,128)S(1)}, f32[2,6,1,256]{3,1,2,0:T(8,128)S(1)}, u32[]{:S(2)}, u32[]{:S(2)}) collective-permute-start(f32[2,6,1,256]{3,1,2,0:T(8,128)S(1)} %slice.185), channel_id=1, source_target_pairs={{1,0},{3,2},{5,4},{7,6},{9,8},{11,10},{13,12},{15,14},{17,16},{19,... | collective-permute-start | bytes 36872 | tf_op jit(solution)/shard_map/ppermute | solution.py:24
  86.1 34.6 %copy-start.14 = (f32[4,1,8,128]{3,2,1,0:T(8,128)S(1)}, f32[4,1,8,128]{3,2,1,0:T(8,128)}, u32[]{:S(2)}) copy-start(f32[4,1,8,128]{3,2,1,0:T(8,128)} %param.18) | copy-start | bytes 49156
  86.1 34.6 %copy-start.15 = (s32[4,1024]{1,0:T(4,128)S(1)}, s32[4,1024]{1,0:T(4,128)}, u32[]{:S(2)}) copy-start(s32[4,1024]{1,0:T(4,128)} %param.25) | copy-start | bytes 49156
  86.2 29.8 %collective-permute-start.9 = (f32[2,1,32,256]{3,2,1,0:T(8,128)S(1)}, f32[2,1,32,256]{3,2,1,0:T(8,128)S(1)}, u32[]{:S(2)}, u32[]{:S(2)}) collective-permute-start(f32[2,1,32,256]{3,2,1,0:T(8,128)S(1)} %get-tuple-element.128), channel_id=1, source_target_pairs={{2,0},{3,1},{6,4},{7,5},{10,8},{11,9},{14,12},{15,13},{18,16},{19,... | collective-permute-start | bytes 196616 | tf_op jit(solution)/shard_map/ppermute | solution.py:24
  87.5 28.5 %collective-permute-start.8 = (f32[2,1,32,256]{3,2,1,0:T(8,128)S(1)}, f32[2,1,32,256]{3,2,1,0:T(8,128)S(1)}, u32[]{:S(2)}, u32[]{:S(2)}) collective-permute-start(f32[2,1,32,256]{3,2,1,0:T(8,128)S(1)} %get-tuple-element.127), channel_id=1, source_target_pairs={{0,2},{1,3},{4,6},{5,7},{8,10},{9,11},{12,14},{13,15},{16,18},{17,... | collective-permute-start | bytes 196616 | tf_op jit(solution)/shard_map/ppermute | solution.py:22
  92.0 28.6 %all-to-all-start.1 = ((f32[4,32,256]{2,0,1:T(4,128)}), f32[4,32,256]{2,0,1:T(4,128)S(1)}, u32[]{:S(2)}, u32[]{:S(2)}) async-start(f32[4,32,256]{2,0,1:T(4,128)} %multiply_subtract_fusion.3), calls=%async_computation.1 | async-start | bytes 262144 | tf_op jit(solution)/shard_map/all_to_all | solution.py:159
  116.3 61.0 %collective-permute-start.11 = (f32[2,6,1,256]{3,1,2,0:T(8,128)S(1)}, f32[2,6,1,256]{3,1,2,0:T(8,128)S(1)}, u32[]{:S(2)}, u32[]{:S(2)}) collective-permute-start(f32[2,6,1,256]{3,1,2,0:T(8,128)S(1)} %slice.193), channel_id=1, source_target_pairs={{0,1},{2,3},{4,5},{6,7},{8,9},{10,11},{12,13},{14,15},{16,17},{18,... | collective-permute-start | bytes 36872 | tf_op jit(solution)/shard_map/ppermute | solution.py:22
  119.3 13.9 %collective-permute-start.10 = (f32[2,6,1,256]{1,3,2,0:T(8,128)}, f32[2,6,1,256]{1,3,2,0:T(8,128)}, u32[]{:S(2)}, u32[]{:S(2)}) collective-permute-start(f32[2,6,1,256]{1,3,2,0:T(8,128)} %copy.197), channel_id=1, source_target_pairs={{1,0},{3,2},{5,4},{7,6},{9,8},{11,10},{13,12},{15,14},{17,16},{19,... | collective-permute-start | bytes 36872 | tf_op jit(solution)/shard_map/ppermute | solution.py:24
  128.7 41.3 %all-to-all-start.2 = ((f32[4,1,8192]{2,1,0:T(1,128)}), f32[4,1,8192]{2,1,0:T(1,128)S(1)}, u32[]{:S(2)}, u32[]{:S(2)}) async-start(f32[4,1,8192]{2,1,0:T(1,128)} %reshape.118), calls=%async_computation.2 | async-start | bytes 262144 | tf_op jit(solution)/shard_map/all_to_all | solution.py:141
  180.0 27.6 %collective-permute-start.13 = (f32[2,1,32,256]{3,2,1,0:T(8,128)S(1)}, f32[2,1,32,256]{3,2,1,0:T(8,128)S(1)}, u32[]{:S(2)}, u32[]{:S(2)}) collective-permute-start(f32[2,1,32,256]{3,2,1,0:T(8,128)S(1)} %get-tuple-element.124), channel_id=1, source_target_pairs={{2,0},{3,1},{6,4},{7,5},{10,8},{11,9},{14,12},{15,13},{18,16},{19,... | collective-permute-start | bytes 196616 | tf_op jit(solution)/shard_map/ppermute | solution.py:24
  181.3 26.3 %collective-permute-start.12 = (f32[2,1,32,256]{3,2,1,0:T(8,128)S(1)}, f32[2,1,32,256]{3,2,1,0:T(8,128)S(1)}, u32[]{:S(2)}, u32[]{:S(2)}) collective-permute-start(f32[2,1,32,256]{3,2,1,0:T(8,128)S(1)} %get-tuple-element.123), channel_id=1, source_target_pairs={{0,2},{1,3},{4,6},{5,7},{8,10},{9,11},{12,14},{13,15},{16,18},{17,... | collective-permute-start | bytes 196616 | tf_op jit(solution)/shard_map/ppermute | solution.py:22
  187.2 30.4 %all-to-all-start.3 = ((f32[4,32,256]{2,0,1:T(4,128)}), f32[4,32,256]{2,0,1:T(4,128)S(1)}, u32[]{:S(2)}, u32[]{:S(2)}) async-start(f32[4,32,256]{2,0,1:T(4,128)} %multiply_subtract_fusion.1), calls=%async_computation.3 | async-start | bytes 262144 | tf_op jit(solution)/shard_map/all_to_all | solution.py:159
  207.9 5.8 %collective-permute-start.15 = (f32[2,6,1,256]{3,1,2,0:T(8,128)S(1)}, f32[2,6,1,256]{3,1,2,0:T(8,128)S(1)}, u32[]{:S(2)}, u32[]{:S(2)}) collective-permute-start(f32[2,6,1,256]{3,1,2,0:T(8,128)S(1)} %slice.201), channel_id=1, source_target_pairs={{1,0},{3,2},{5,4},{7,6},{9,8},{11,10},{13,12},{15,14},{17,16},{19,... | collective-permute-start | bytes 36872 | tf_op jit(solution)/shard_map/ppermute | solution.py:24
  209.4 4.2 %collective-permute-start.14 = (f32[2,6,1,256]{1,3,2,0:T(8,128)S(1)}, f32[2,6,1,256]{1,3,2,0:T(8,128)S(1)}, u32[]{:S(2)}, u32[]{:S(2)}) collective-permute-start(f32[2,6,1,256]{1,3,2,0:T(8,128)S(1)} %copy.201), channel_id=1, source_target_pairs={{0,1},{2,3},{4,5},{6,7},{8,9},{10,11},{12,13},{14,15},{16,17},{18,... | collective-permute-start | bytes 36872 | tf_op jit(solution)/shard_map/ppermute | solution.py:22
  (13 other events, 152.4 us)
where the time goes:
time: 257 us; the launch traced here: 256 us
  blocking collectives  123 us (48%)
  starting transfers between devices  57.3 us (22%)
  local copies, waits for them, and re-layouts  34.9 us (14%)
  other arithmetic  15.8 us (6%)
  between operations  12.1 us (5%)
  matrix products  8.66 us (3%)
  waiting for transfers between devices  3.97 us (2%)
    psum x2, blocking collectives, on_device(): lax.psum((primal_sq, dual_sq), ('pipe', 'hour', 'seg'))  65.5 us
    all_gather x4, blocking collectives, other_half(): lax.all_gather(edge_row[:, None, :], ('pipe', 'seg'), axis=1, tiled=True)  57.8 us
    ppermute x8, starting transfers between devices, padded(): lax.ppermute(tail, axis, [(i, (i + 1) % count) for i in range(ends)])  27.9 us
    unnamed x55, local copies, waits for them, and re-layouts  17 us
    all_to_all x2, starting transfers between devices, on_device(): lax.all_to_all(hour_spread, 'pipe', split_axis=2, concat_axis=1, tiled=True)  10.8 us
    ppermute x8, starting transfers between devices, padded(): lax.ppermute(head, axis, [((i + 1) % count, i) for i in range(ends)])  10.6 us
    all_to_all x2, starting transfers between devices, on_device(): lax.all_to_all(pack_bar, 'pipe', split_axis=1, concat_axis=2, tiled=True)  7.96 us
  transfers between devices with their start and end apart: 20, of which 3 were waited for; matrix products, arithmetic and copies ran while one was open for 16% of the time, Pallas kernels for 0%

commit v1 on v0

--- a/solution.py
+++ b/solution.py
@@ -138,7 +138,12 @@
         next_seg = jnp.concatenate([mass_dual[:, 1:, :], last_row[:, None, :]], axis=1)
         grad_flow = mass_dual - next_seg + friction * momentum_dual
         hour_spread = spread_local(contract_now, contract_map)
-        spread = lax.all_to_all(hour_spread, "pipe", split_axis=2, concat_axis=1, tiled=True)
+        spread = jnp.concatenate(
+            lax.all_to_all(
+                jnp.stack(jnp.split(hour_spread, lax.axis_size("pipe"), axis=2)), "pipe", 0, 0
+            ),
+            axis=1,
+        )
         grad_pack = mass_dual - later_hour - momentum_dual + before_seg + share_scale * spread
         grad_flow, grad_pack = (grad_flow, grad_pack)
         flow_next = jnp.clip(

time: 257 us -> 222 us (0.86)
  local copies, waits for them, and re-layouts: 34.9 us -> 11.4 us
  other arithmetic: 15.8 us -> 6.76 us
  starting transfers between devices: 57.3 us -> 50.2 us
  waiting for transfers between devices: 3.97 us -> 7.97 us
    unnamed x55 -> x37, local copies, waits for them, and re-layouts: 17 us -> 2.16 us
    ppermute x8, starting transfers between devices: 27.9 us -> 23.2 us  [padded(): lax.ppermute(tail, axis, [(i, (i + 1) % count) for i in range(ends)])]
    ppermute x8, waiting for transfers between devices: 2.83 us -> 7.35 us  [padded(): lax.ppermute(head, axis, [((i + 1) % count, i) for i in range(ends)])]
    mul x2 -> x0, local copies, waits for them, and re-layouts: 3.8 us -> none  [on_device(): share_scale * spread]
    mul x2 -> x0, other arithmetic: 3.59 us -> none  [on_device(): share_scale * spread]
  transfers between devices with their start and end apart: 20 -> 20, of which waited for: 3 -> 5; matrix products, arithmetic and copies ran while one was open for 16% -> 10% of each run, Pallas kernels for 0% -> 0%
where the time goes in v1:
time: 222 us; the launch traced here: 221 us
  blocking collectives  124 us (56%)
  starting transfers between devices  50.2 us (23%)
  between operations  11.8 us (5%)
  local copies, waits for them, and re-layouts  11.4 us (5%)
  matrix products  8.66 us (4%)
  waiting for transfers between devices  7.97 us (4%)
  other arithmetic  6.76 us (3%)
    psum x2, blocking collectives, on_device(): lax.psum((primal_sq, dual_sq), ('pipe', 'hour', 'seg'))  67 us
    all_gather x4, blocking collectives, other_half(): lax.all_gather(edge_row[:, None, :], ('pipe', 'seg'), axis=1, tiled=True)  57.4 us
    ppermute x8, starting transfers between devices, padded(): lax.ppermute(tail, axis, [(i, (i + 1) % count) for i in range(ends)])  23.2 us
    ppermute x8, starting transfers between devices, padded(): lax.ppermute(head, axis, [((i + 1) % count, i) for i in range(ends)])  10.3 us
    all_to_all x2, starting transfers between devices, on_device(): lax.all_to_all(jnp.stack(jnp.split(hour_spread, lax.axis_size('pipe'), ax...  9.35 us
    ppermute x8, waiting for transfers between devices, padded(): lax.ppermute(head, axis, [((i + 1) % count, i) for i in range(ends)])  7.35 us
    all_to_all x2, starting transfers between devices, on_device(): lax.all_to_all(pack_bar, 'pipe', split_axis=1, concat_axis=2, tiled=True)  7.26 us
    dot_general x2, matrix products, add_block(): jnp.einsum('hsp,hpc->hsc', partial_value, onehot, precision=lax.Precision...  4.64 us
  transfers between devices with their start and end apart: 20, of which 5 were waited for; matrix products, arithmetic and copies ran while one was open for 10% of the time, Pallas kernels for 0%

profile of v1, /device:TPU:0, one launch (start us, length us, event | category | flops | bytes accessed | tf_op | source)
XLA Modules:
  0.0 221.2 jit_solution(16382541856927222528)
XLA Ops:
  1.5 4.8 %collective-permute-start = (f32[2,1,32,256]{3,2,1,0:T(8,128)S(1)}, f32[2,1,32,256]{3,2,1,0:T(8,128)S(1)}, u32[]{:S(2)}, u32[]{:S(2)}) collective-permute-start(f32[2,1,32,256]{3,2,1,0:T(8,128)S(1)} %get-tuple-element.149), channel_id=1, source_target_pairs={{0,2},{1,3},{4,6},{5,7},{8,10},{9,11},{12,14},{13,15},{16,18},{17,... | collective-permute-start | bytes 196616 | tf_op jit(solution)/shard_map/ppermute | solution.py:22
  7.6 2.2 fusion.4
  10.6 4.9 %all-to-all-start = ((f32[4,4,8,256]{3,2,1,0:T(8,128)}), f32[4,4,8,256]{3,2,1,0:T(8,128)S(1)}, u32[]{:S(2)}, u32[]{:S(2)}) async-start(f32[4,4,8,256]{3,2,1,0:T(8,128)} %pad_maximum_fusion.24), calls=%async_computation | async-start | bytes 262144 | tf_op jit(solution)/shard_map/all_to_all | solution.py:142
  15.5 4.3 %scatter_custom_fusion = s32[1024]{0:T(1024)S(1)} fusion(s32[1024]{0:T(1024)S(1)} %compare_select_fusion, s32[1024]{0:T(1024)S(1)} %iota.14, s32[]{:T(128)} %constant.26.clone.1), kind=kCustom, calls=%fused_computation.177 | custom fusion | bytes 4100 | tf_op jit(solution)/shard_map/scatter | solution.py:122
  21.6 15.1 %all_gather.12 = f32[4,8,256]{2,0,1:T(4,128)S(1)} all-gather(f32[4,1,256]{2,0,1:T(4,128)S(1)} %copy.159), channel_id=1, replica_groups=mesh['groups'=2,'pipe'=4,'hour'=2,'seg'=2] {'pipe','seg'}, dimensions={1}, use_global_device_ids=true | all-gather | bytes 36864 | tf_op jit(solution)/shard_map/all_gather | solution.py:36
  37.8 2.2 collective-permute-start.3
  41.6 4.5 %collective-permute-start.4 = (f32[2,1,32,256]{3,2,1,0:T(8,128)S(1)}, f32[2,1,32,256]{3,2,1,0:T(8,128)S(1)}, u32[]{:S(2)}, u32[]{:S(2)}) collective-permute-start(f32[2,1,32,256]{3,2,1,0:T(8,128)S(1)} %get-tuple-element.145), channel_id=1, source_target_pairs={{0,2},{1,3},{4,6},{5,7},{8,10},{9,11},{12,14},{13,15},{16,18},{17,... | collective-permute-start | bytes 196616 | tf_op jit(solution)/shard_map/ppermute | solution.py:22
  48.2 3.9 %all-to-all-start.1 = ((f32[4,32,256]{2,0,1:T(4,128)}), f32[4,32,256]{2,0,1:T(4,128)S(1)}, u32[]{:S(2)}, u32[]{:S(2)}) async-start(f32[4,32,256]{2,0,1:T(4,128)} %copy.144), calls=%async_computation.1 | async-start | bytes 262144 | tf_op jit(solution)/shard_map/all_to_all | solution.py:164
  52.5 1.6 collective-permute-start.6
  54.1 14.3 %all_gather.13 = f32[4,8,256]{2,0,1:T(4,128)S(1)} all-gather(f32[4,1,256]{2,0,1:T(4,128)S(1)} %copy.141), channel_id=1, replica_groups=mesh['groups'=2,'pipe'=4,'hour'=2,'seg'=2] {'pipe','seg'}, dimensions={1}, use_global_device_ids=true | all-gather | bytes 36864 | tf_op jit(solution)/shard_map/all_gather | solution.py:36
  70.8 1.5 collective-permute-done.7
  73.1 4.4 %collective-permute-start.8 = (f32[2,1,32,256]{3,2,1,0:T(8,128)S(1)}, f32[2,1,32,256]{3,2,1,0:T(8,128)S(1)}, u32[]{:S(2)}, u32[]{:S(2)}) collective-permute-start(f32[2,1,32,256]{3,2,1,0:T(8,128)S(1)} %get-tuple-element.143), channel_id=1, source_target_pairs={{0,2},{1,3},{4,6},{5,7},{8,10},{9,11},{12,14},{13,15},{16,18},{17,... | collective-permute-start | bytes 196616 | tf_op jit(solution)/shard_map/ppermute | solution.py:22
  80.2 14.0 %all_gather.14 = f32[4,8,256]{2,0,1:T(4,128)S(1)} all-gather(f32[4,1,256]{2,0,1:T(4,128)S(1)} %copy.147), channel_id=1, replica_groups=mesh['groups'=2,'pipe'=4,'hour'=2,'seg'=2] {'pipe','seg'}, dimensions={1}, use_global_device_ids=true | all-gather | bytes 36864 | tf_op jit(solution)/shard_map/all_gather | solution.py:36
  98.0 3.0 %collective-permute-start.11 = (f32[2,6,1,256]{3,2,1,0:T(1,128)S(1)}, f32[2,6,1,256]{3,2,1,0:T(1,128)S(1)}, u32[]{:S(2)}, u32[]{:S(2)}) collective-permute-start(f32[2,6,1,256]{3,2,1,0:T(1,128)S(1)} %get-tuple-element.133), channel_id=1, source_target_pairs={{0,1},{2,3},{4,5},{6,7},{8,9},{10,11},{12,13},{14,15},{16,17},{18,... | collective-permute-start | bytes 36872 | tf_op jit(solution)/shard_map/ppermute | solution.py:22
  101.1 2.2 %fusion.79 = (f32[]{:T(128)}, f32[4,8,128]{2,1,0:T(8,128)S(1)}) fusion(f32[4,1,8,128]{3,2,1,0:T(8,128)S(1)} %copy-done.11, f32[4,8,1024]{2,1,0:T(8,128)S(1)} %bitcast.252, s32[4,1024]{1,0:T(4,128)S(1)} %copy-done.12, f32[4,1,8,128]{3,2,1,0:T(8,128)S(1)} %copy-done.13), kind=kOutput, calls=%fused_computation.154 | convolution fusion | flops 50884608 | bytes 196612 | tf_op jit(solution)/shard_map/while/body/eval_jaxpr/hsp,hpc->hsc/dot_general | solution.py:55
  103.3 1.8 fusion.1
  105.9 4.5 %all-to-all-start.2 = ((f32[4,4,8,256]{3,2,1,0:T(8,128)}), f32[4,4,8,256]{3,2,1,0:T(8,128)S(1)}, u32[]{:S(2)}, u32[]{:S(2)}) async-start(f32[4,4,8,256]{3,2,1,0:T(8,128)} %pad_maximum_fusion.25), calls=%async_computation.2 | async-start | bytes 262144 | tf_op jit(solution)/shard_map/all_to_all | solution.py:142
  111.2 34.3 %all-reduce.1 = (f32[]{:T(128)}, f32[]{:T(128)}) all-reduce(f32[]{:T(128)S(6)} %add.153, f32[]{:T(128)S(6)} %add.155), channel_id=1, replica_groups=mesh['groups'=2,'pipe'=4,'hour'=2,'seg'=2] {'pipe','hour','seg'}, use_global_device_ids=true, to_apply=%region_5.7 | all-reduce | flops 2 | bytes 16 | tf_op jit(solution)/shard_map/psum | solution.py:176
  151.8 4.1 %collective-permute-done.13 = f32[2,1,32,256]{3,2,1,0:T(8,128)S(1)} collective-permute-done((f32[2,1,32,256]{3,2,1,0:T(8,128)S(1)}, f32[2,1,32,256]{3,2,1,0:T(8,128)S(1)}, u32[]{:S(2)}, u32[]{:S(2)}) %collective-permute-start.13) | collective-permute-done | bytes 65568 | tf_op jit(solution)/shard_map/ppermute | solution.py:24
  157.4 14.0 %all_gather.15 = f32[4,8,256]{2,0,1:T(4,128)S(1)} all-gather(f32[4,1,256]{2,0,1:T(4,128)S(1)} %copy.152), channel_id=1, replica_groups=mesh['groups'=2,'pipe'=4,'hour'=2,'seg'=2] {'pipe','seg'}, dimensions={1}, use_global_device_ids=true | all-gather | bytes 36864 | tf_op jit(solution)/shard_map/all_gather | solution.py:36
  172.4 3.3 %all-to-all-start.3 = ((f32[4,32,256]{2,0,1:T(4,128)}), f32[4,32,256]{2,0,1:T(4,128)S(1)}, u32[]{:S(2)}, u32[]{:S(2)}) async-start(f32[4,32,256]{2,0,1:T(4,128)} %copy.155), calls=%async_computation.3 | async-start | bytes 262144 | tf_op jit(solution)/shard_map/all_to_all | solution.py:164
  178.5 1.5 collective-permute-done.15
  182.8 2.4 %multiply_reduce_fusion.8 = (f32[]{:T(128)}, f32[4,8,128]{2,1,0:T(8,128)}) fusion(f32[4,8,128]{2,1,0:T(8,128)S(1)} %get-tuple-element.160, f32[4,8,1024]{2,1,0:T(8,128)S(1)} %bitcast.251, s32[4,1024]{1,0:T(4,128)S(1)} %copy-done.12, f32[4,1,8,128]{3,2,1,0:T(8,128)S(1)} %copy-done.13, f32[]{:T(128)S(6)} %mul.150), kind=kOutput, calls=%fused_computation.155 | convolution fusion | flops 50884608 | bytes 196616 | tf_op jit(solution)/shard_map/while/body/eval_jaxpr/hsp,hpc->hsc/dot_general | solution.py:55
  185.9 32.7 %all-reduce = (f32[]{:T(128)}, f32[]{:T(128)}) all-reduce(f32[]{:T(128)S(6)} %add.167, f32[]{:T(128)S(6)} %add.169), channel_id=1, replica_groups=mesh['groups'=2,'pipe'=4,'hour'=2,'seg'=2] {'pipe','hour','seg'}, use_global_device_ids=true, to_apply=%region_12.14 | all-reduce | flops 2 | bytes 16 | tf_op jit(solution)/shard_map/psum | solution.py:176
  (119 shorter events, 27.5 us)
Async XLA Ops:
  1.5 18.7 %collective-permute-start = (f32[2,1,32,256]{3,2,1,0:T(8,128)S(1)}, f32[2,1,32,256]{3,2,1,0:T(8,128)S(1)}, u32[]{:S(2)}, u32[]{:S(2)}) collective-permute-start(f32[2,1,32,256]{3,2,1,0:T(8,128)S(1)} %get-tuple-element.149), channel_id=1, source_target_pairs={{0,2},{1,3},{4,6},{5,7},{8,10},{9,11},{12,14},{13,15},{16,18},{17,... | collective-permute-start | bytes 196616 | tf_op jit(solution)/shard_map/ppermute | solution.py:22
  6.3 13.8 %collective-permute-start.1 = (f32[2,1,32,256]{3,2,1,0:T(8,128)S(1)}, f32[2,1,32,256]{3,2,1,0:T(8,128)S(1)}, u32[]{:S(2)}, u32[]{:S(2)}) collective-permute-start(f32[2,1,32,256]{3,2,1,0:T(8,128)S(1)} %get-tuple-element.150), channel_id=1, source_target_pairs={{2,0},{3,1},{6,4},{7,5},{10,8},{11,9},{14,12},{15,13},{18,16},{19,... | collective-permute-start | bytes 196616 | tf_op jit(solution)/shard_map/ppermute | solution.py:24
  9.8 10.1 %copy-start.8 = (s32[32,256]{1,0:T(8,128)S(1)}, s32[32,256]{1,0:T(8,128)}, u32[]{:S(2)}) copy-start(s32[32,256]{1,0:T(8,128)} %param.23) | copy-start | bytes 98308
  9.8 10.1 %copy-start.10 = (f32[16]{0:T(128)S(1)}, f32[16]{0:T(128)}, u32[]{:S(2)}) copy-start(f32[16]{0:T(128)} %param.22) | copy-start | bytes 196
  9.9 10.3 %copy-start.1 = (f32[4,32,256]{2,1,0:T(8,128)S(1)}, f32[4,32,256]{2,1,0:T(8,128)}, u32[]{:S(2)}) copy-start(f32[4,32,256]{2,1,0:T(8,128)} %param.17) | copy-start | bytes 393220
  10.6 30.2 %all-to-all-start = ((f32[4,4,8,256]{3,2,1,0:T(8,128)}), f32[4,4,8,256]{3,2,1,0:T(8,128)S(1)}, u32[]{:S(2)}, u32[]{:S(2)}) async-start(f32[4,4,8,256]{3,2,1,0:T(8,128)} %pad_maximum_fusion.24), calls=%async_computation | async-start | bytes 262144 | tf_op jit(solution)/shard_map/all_to_all | solution.py:142
  20.3 19.6 %collective-permute-start.2 = (f32[2,6,1,256]{1,3,2,0:T(8,128)S(1)}, f32[2,6,1,256]{1,3,2,0:T(8,128)S(1)}, u32[]{:S(2)}, u32[]{:S(2)}) collective-permute-start(f32[2,6,1,256]{1,3,2,0:T(8,128)S(1)} %copy.158), channel_id=1, source_target_pairs={{1,0},{3,2},{5,4},{7,6},{9,8},{11,10},{13,12},{15,14},{17,16},{19,... | collective-permute-start | bytes 36872 | tf_op jit(solution)/shard_map/ppermute | solution.py:24
  37.8 3.0 %collective-permute-start.3 = (f32[2,6,1,256]{3,2,1,0:T(1,128)S(1)}, f32[2,6,1,256]{3,2,1,0:T(1,128)S(1)}, u32[]{:S(2)}, u32[]{:S(2)}) collective-permute-start(f32[2,6,1,256]{3,2,1,0:T(1,128)S(1)} %get-tuple-element.137), channel_id=1, source_target_pairs={{0,1},{2,3},{4,5},{6,7},{8,9},{10,11},{12,13},{14,15},{16,17},{18,... | collective-permute-start | bytes 36872 | tf_op jit(solution)/shard_map/ppermute | solution.py:22
  41.6 10.6 %collective-permute-start.4 = (f32[2,1,32,256]{3,2,1,0:T(8,128)S(1)}, f32[2,1,32,256]{3,2,1,0:T(8,128)S(1)}, u32[]{:S(2)}, u32[]{:S(2)}) collective-permute-start(f32[2,1,32,256]{3,2,1,0:T(8,128)S(1)} %get-tuple-element.145), channel_id=1, source_target_pairs={{0,2},{1,3},{4,6},{5,7},{8,10},{9,11},{12,14},{13,15},{16,18},{17,... | collective-permute-start | bytes 196616 | tf_op jit(solution)/shard_map/ppermute | solution.py:22
  46.2 6.2 %collective-permute-start.5 = (f32[2,1,32,256]{3,2,1,0:T(8,128)S(1)}, f32[2,1,32,256]{3,2,1,0:T(8,128)S(1)}, u32[]{:S(2)}, u32[]{:S(2)}) collective-permute-start(f32[2,1,32,256]{3,2,1,0:T(8,128)S(1)} %get-tuple-element.146), channel_id=1, source_target_pairs={{2,0},{3,1},{6,4},{7,5},{10,8},{11,9},{14,12},{15,13},{18,16},{19,... | collective-permute-start | bytes 196616 | tf_op jit(solution)/shard_map/ppermute | solution.py:24
  48.2 52.8 %all-to-all-start.1 = ((f32[4,32,256]{2,0,1:T(4,128)}), f32[4,32,256]{2,0,1:T(4,128)S(1)}, u32[]{:S(2)}, u32[]{:S(2)}) async-start(f32[4,32,256]{2,0,1:T(4,128)} %copy.144), calls=%async_computation.1 | async-start | bytes 262144 | tf_op jit(solution)/shard_map/all_to_all | solution.py:164
  52.5 18.1 %collective-permute-start.6 = (f32[2,6,1,256]{1,3,2,0:T(8,128)S(1)}, f32[2,6,1,256]{1,3,2,0:T(8,128)S(1)}, u32[]{:S(2)}, u32[]{:S(2)}) collective-permute-start(f32[2,6,1,256]{1,3,2,0:T(8,128)S(1)} %copy.161), channel_id=1, source_target_pairs={{0,1},{2,3},{4,5},{6,7},{8,9},{10,11},{12,13},{14,15},{16,17},{18,... | collective-permute-start | bytes 36872 | tf_op jit(solution)/shard_map/ppermute | solution.py:22
  69.3 3.1 %collective-permute-start.7 = (f32[2,6,1,256]{3,2,1,0:T(1,128)S(1)}, f32[2,6,1,256]{3,2,1,0:T(1,128)S(1)}, u32[]{:S(2)}, u32[]{:S(2)}) collective-permute-start(f32[2,6,1,256]{3,2,1,0:T(1,128)S(1)} %get-tuple-element.136), channel_id=1, source_target_pairs={{1,0},{3,2},{5,4},{7,6},{9,8},{11,10},{13,12},{15,14},{17,16},{19,... | collective-permute-start | bytes 36872 | tf_op jit(solution)/shard_map/ppermute | solution.py:24
  73.1 23.4 %collective-permute-start.8 = (f32[2,1,32,256]{3,2,1,0:T(8,128)S(1)}, f32[2,1,32,256]{3,2,1,0:T(8,128)S(1)}, u32[]{:S(2)}, u32[]{:S(2)}) collective-permute-start(f32[2,1,32,256]{3,2,1,0:T(8,128)S(1)} %get-tuple-element.143), channel_id=1, source_target_pairs={{0,2},{1,3},{4,6},{5,7},{8,10},{9,11},{12,14},{13,15},{16,18},{17,... | collective-permute-start | bytes 196616 | tf_op jit(solution)/shard_map/ppermute | solution.py:22
  77.5 19.0 %collective-permute-start.9 = (f32[2,1,32,256]{3,2,1,0:T(8,128)S(1)}, f32[2,1,32,256]{3,2,1,0:T(8,128)S(1)}, u32[]{:S(2)}, u32[]{:S(2)}) collective-permute-start(f32[2,1,32,256]{3,2,1,0:T(8,128)S(1)} %get-tuple-element.144), channel_id=1, source_target_pairs={{2,0},{3,1},{6,4},{7,5},{10,8},{11,9},{14,12},{15,13},{18,16},{19,... | collective-permute-start | bytes 196616 | tf_op jit(solution)/shard_map/ppermute | solution.py:24
  94.4 6.7 %copy-start.11 = (f32[4,1,8,128]{3,2,1,0:T(8,128)S(1)}, f32[4,1,8,128]{3,2,1,0:T(8,128)}, u32[]{:S(2)}) copy-start(f32[4,1,8,128]{3,2,1,0:T(8,128)} %param.18) | copy-start | bytes 49156
  96.7 13.7 %collective-permute-start.10 = (f32[2,6,1,256]{1,3,2,0:T(8,128)S(1)}, f32[2,6,1,256]{1,3,2,0:T(8,128)S(1)}, u32[]{:S(2)}, u32[]{:S(2)}) collective-permute-start(f32[2,6,1,256]{1,3,2,0:T(8,128)S(1)} %copy.163), channel_id=1, source_target_pairs={{1,0},{3,2},{5,4},{7,6},{9,8},{11,10},{13,12},{15,14},{17,16},{19,... | collective-permute-start | bytes 36872 | tf_op jit(solution)/shard_map/ppermute | solution.py:24
  98.0 49.0 %collective-permute-start.11 = (f32[2,6,1,256]{3,2,1,0:T(1,128)S(1)}, f32[2,6,1,256]{3,2,1,0:T(1,128)S(1)}, u32[]{:S(2)}, u32[]{:S(2)}) collective-permute-start(f32[2,6,1,256]{3,2,1,0:T(1,128)S(1)} %get-tuple-element.133), channel_id=1, source_target_pairs={{0,1},{2,3},{4,5},{6,7},{8,9},{10,11},{12,13},{14,15},{16,17},{18,... | collective-permute-start | bytes 36872 | tf_op jit(solution)/shard_map/ppermute | solution.py:22
  105.9 41.1 %all-to-all-start.2 = ((f32[4,4,8,256]{3,2,1,0:T(8,128)}), f32[4,4,8,256]{3,2,1,0:T(8,128)S(1)}, u32[]{:S(2)}, u32[]{:S(2)}) async-start(f32[4,4,8,256]{3,2,1,0:T(8,128)} %pad_maximum_fusion.25), calls=%async_computation.2 | async-start | bytes 262144 | tf_op jit(solution)/shard_map/all_to_all | solution.py:142
  148.4 3.4 %collective-permute-start.12 = (f32[2,1,32,256]{3,2,1,0:T(8,128)S(1)}, f32[2,1,32,256]{3,2,1,0:T(8,128)S(1)}, u32[]{:S(2)}, u32[]{:S(2)}) collective-permute-start(f32[2,1,32,256]{3,2,1,0:T(8,128)S(1)} %get-tuple-element.139), channel_id=1, source_target_pairs={{0,2},{1,3},{4,6},{5,7},{8,10},{9,11},{12,14},{13,15},{16,18},{17,... | collective-permute-start | bytes 196616 | tf_op jit(solution)/shard_map/ppermute | solution.py:22
  149.7 6.2 %collective-permute-start.13 = (f32[2,1,32,256]{3,2,1,0:T(8,128)S(1)}, f32[2,1,32,256]{3,2,1,0:T(8,128)S(1)}, u32[]{:S(2)}, u32[]{:S(2)}) collective-permute-start(f32[2,1,32,256]{3,2,1,0:T(8,128)S(1)} %get-tuple-element.140), channel_id=1, source_target_pairs={{2,0},{3,1},{6,4},{7,5},{10,8},{11,9},{14,12},{15,13},{18,16},{19,... | collective-permute-start | bytes 196616 | tf_op jit(solution)/shard_map/ppermute | solution.py:24
  156.1 22.2 %collective-permute-start.14 = (f32[2,6,1,256]{1,3,2,0:T(8,128)S(1)}, f32[2,6,1,256]{1,3,2,0:T(8,128)S(1)}, u32[]{:S(2)}, u32[]{:S(2)}) collective-permute-start(f32[2,6,1,256]{1,3,2,0:T(8,128)S(1)} %copy.165), channel_id=1, source_target_pairs={{0,1},{2,3},{4,5},{6,7},{8,9},{10,11},{12,13},{14,15},{16,17},{18,... | collective-permute-start | bytes 36872 | tf_op jit(solution)/shard_map/ppermute | solution.py:22
  172.4 10.4 %all-to-all-start.3 = ((f32[4,32,256]{2,0,1:T(4,128)}), f32[4,32,256]{2,0,1:T(4,128)S(1)}, u32[]{:S(2)}, u32[]{:S(2)}) async-start(f32[4,32,256]{2,0,1:T(4,128)} %copy.155), calls=%async_computation.3 | async-start | bytes 262144 | tf_op jit(solution)/shard_map/all_to_all | solution.py:164
  177.0 3.1 %collective-permute-start.15 = (f32[2,6,1,256]{3,2,1,0:T(1,128)S(1)}, f32[2,6,1,256]{3,2,1,0:T(1,128)S(1)}, u32[]{:S(2)}, u32[]{:S(2)}) collective-permute-start(f32[2,6,1,256]{3,2,1,0:T(1,128)S(1)} %get-tuple-element.131), channel_id=1, source_target_pairs={{1,0},{3,2},{5,4},{7,6},{9,8},{11,10},{13,12},{15,14},{17,16},{19,... | collective-permute-start | bytes 36872 | tf_op jit(solution)/shard_map/ppermute | solution.py:24
  (10 other events, 42.0 us)
